TPU v7x, 256 devices: a whole 4x4x8 slice. The times are simulated.
256 devices in a mesh: tensor: 8 (over x, z_lo), member: 4 (over z_hi), image: 8 (over y, core).
Axes of the slice: x: 4, y: 4, z: 8 (z_hi: 4, z_lo: 2; z = z_hi * 2 + z_lo), core: 2. Of those that a mesh axis runs over, the one named last changes fastest.
Arguments:
- acts: bfloat16 [4, 8, 1024, 3200], P('member', 'image', 'tensor'), may hold values from -12 to 12
- perturb: bfloat16 [1024, 3200], P(('tensor', 'member', 'image')), may hold values from -1.796875 to 1.796875
- dy: bfloat16 [4, 8, 1024, 3200], P('member', 'image', 'tensor'), may hold values from -1.5 to 1.5
- norm_gain: float32 [4, 3200], P('member'), may hold values from 0.5 to 1.5
- w_qkv: bfloat16 [4, 3200, 16, 3, 128], P('member', None, 'tensor'), may hold values from -4 to 4
- w_out: bfloat16 [4, 16, 128, 3200], P('member', 'tensor'), may hold values from -0.375 to 0.375
Outputs:
- grad_perturb: float32 [1024, 3200], P(('tensor', 'member', 'image'))
All inputs are finite; a program needn't handle non-finite values.
Results may differ from a plain program's by a relative error of at most 0.013.
The roundings to bfloat16 on the way count: a program that leaves them out, or rounds other values in their place, can miss the bound.
Values may be sent and summed in bfloat16 or wider, within the bound.
No kernel may reach another device: no remote copies, remote signals or barrier semaphores. Data moves between devices by JAX's collectives and lax.ppermute only.
A program may use at most 128 MiB of HBM per device.

v0:
```python
import math
import jax
import jax.numpy as jnp
from jax import lax
from jax.sharding import PartitionSpec as P


def normalize(row_block):
    floats = row_block.astype(jnp.float32)
    spread = jnp.sqrt(jnp.mean(floats * floats, axis=-1, keepdims=True) + 1e-06)
    return (floats / spread, spread)


def norm_back(normed_grad, row_block, gains, upstream):
    scaled_rows, spread = normalize(row_block)
    weighted = gains * normed_grad
    centre = jnp.mean(scaled_rows * weighted, axis=-1, keepdims=True)
    return upstream.astype(jnp.float32) + (weighted - scaled_rows * centre) / spread


def head_grads(query, keys, values, upstream, score_scale):
    scores = jnp.einsum("qe,ke->qk", query, keys, preferred_element_type=jnp.float32) * score_scale
    peak = jnp.max(scores, axis=-1, keepdims=True)
    expo = jnp.exp(scores - peak)
    attention = expo / jnp.sum(expo, axis=-1, keepdims=True)
    rounded = attention.astype(jnp.bfloat16)
    through = jnp.einsum("qe,ke->qk", upstream, values, preferred_element_type=jnp.float32)
    value_grad = jnp.einsum(
        "qk,qe->ke", rounded, upstream, preferred_element_type=jnp.float32
    ).astype(jnp.bfloat16)
    centre = jnp.sum(attention * through, axis=-1, keepdims=True)
    score_grad = (attention * (through - centre) * score_scale).astype(jnp.bfloat16)
    query_grad = jnp.einsum(
        "qk,ke->qe", score_grad, keys, preferred_element_type=jnp.float32
    ).astype(jnp.bfloat16)
    key_grad = jnp.einsum(
        "qk,qe->ke", score_grad, query, preferred_element_type=jnp.float32
    ).astype(jnp.bfloat16)
    return (query_grad, key_grad, value_grad)


def on_device(acts, perturb, dy, norm_gain, w_qkv, w_out):
    own_rows = acts[0, 0]
    own_grad = dy[0, 0]
    gains = norm_gain[0]
    features = own_rows.shape[1]
    head_count = w_qkv.shape[2]
    head_size = w_qkv.shape[4]
    w_mat = w_qkv[0].reshape(features, head_count * 3 * head_size)
    w_back = w_out[0].reshape(head_count * head_size, features)
    score_scale = 1.0 / math.sqrt(head_size)
    shared = lax.all_gather(perturb, ("member", "image"), axis=0, tiled=True)
    inputs = (own_rows.astype(jnp.float32) + shared.astype(jnp.float32)).astype(jnp.bfloat16)
    all_inputs = lax.all_gather(inputs, "tensor", axis=0, tiled=True)
    scaled_rows, spread = normalize(all_inputs)
    normed = (scaled_rows * gains).astype(jnp.bfloat16)
    packed = jnp.dot(normed, w_mat, preferred_element_type=jnp.float32).astype(jnp.bfloat16)
    product = lax.dot_general(
        lax.all_gather(own_grad, "tensor", axis=0, tiled=True),
        w_back,
        (((1,), (1,)), ((), ())),
        preferred_element_type=jnp.float32,
    )
    heads_up = product.astype(jnp.bfloat16)
    length = packed.shape[0]
    packed = packed.reshape(length, head_count, 3, head_size)
    heads_up = heads_up.reshape(length, head_count, head_size)
    pieces = []
    for head_number in range(head_count):
        grads = head_grads(
            packed[:, head_number, 0],
            packed[:, head_number, 1],
            packed[:, head_number, 2],
            heads_up[:, head_number],
            score_scale,
        )
        pieces.append(jnp.stack(grads, axis=1))
    packed_back = jnp.stack(pieces, axis=1).reshape(length, head_count * 3 * head_size)
    local_rows = own_rows.shape[0]
    placed = lax.dynamic_update_slice_in_dim(
        jnp.zeros((length, features), jnp.bfloat16),
        own_grad,
        lax.axis_index("tensor") * local_rows,
        0,
    )
    group_part = lax.dot_general(
        packed_back, w_mat, (((1,), (1,)), ((), ())), preferred_element_type=jnp.float32
    )
    normed_grad = lax.optimization_barrier(group_part.astype(jnp.bfloat16)).astype(jnp.float32)
    return lax.psum_scatter(
        norm_back(normed_grad, all_inputs, gains, placed),
        ("tensor", "member", "image"),
        scatter_dimension=0,
        tiled=True,
    )


def solution(mesh):
    in_specs = (
        P("member", "image", "tensor", None),
        P(("tensor", "member", "image"), None),
        P("member", "image", "tensor", None),
        P("member", None),
        P("member", None, "tensor", None, None),
        P("member", "tensor", None, None),
    )
    out_specs = P(("tensor", "member", "image"), None)
    return jax.shard_map(
        on_device, mesh=mesh, in_specs=in_specs, out_specs=out_specs, check_vma=False
    )
```

profile of v0, /device:TPU:2, one launch (start us, length us, event | category | flops | bytes accessed | tf_op | source)
XLA Modules:
  0.0 667.7 jit_solution(2604758338790818520)
XLA Ops:
  6.5 53.6 %all-gather.1 = bf16[32,4,3200]{2,1,0:T(4,128)(2,1)} all-gather(bf16[1,4,3200]{2,1,0:T(4,128)(2,1)} %bitcast.102), channel_id=1, replica_groups=mesh['tensor'=8,'member'=4,'image'=8] {'member','image'}, dimensions={0}, use_global_device_ids=true | all-gather | bytes 844800 | tf_op jit(solution)/shard_map/all_gather | solution.py:52
  60.1 1.5 reshape.36
  61.7 2.2 fusion.14
  64.7 14.2 %copy.8 = bf16[1,3200,2,3,128]{1,4,3,2,0:T(8,128)(2,1)} copy(bf16[1,3200,2,3,128]{4,2,3,1,0:T(2,128)(2,1)} %param.10) | data formatting | bytes 9830400 | tf_op args[4]
  79.0 3.1 broadcast_in_dim.2
  82.1 1.0 bitcast_dynamic-update-slice_fusion
  83.1 111.4 %all-gather.5.cloned.1.call-done = bf16[1024,3200]{1,0:T(8,128)(2,1)} async-done(((bf16[128,3200]{1,0:T(8,128)(2,1)}), bf16[1024,3200]{1,0:T(8,128)(2,1)}) %all-gather.5.cloned.1.call-update) | async-done | bytes 6553616 | tf_op jit(solution)/shard_map/all_gather | solution.py:54
  194.5 4.4 fusion
  199.3 8.0 %fusion.13 = bf16[1024,768]{0,1:T(8,128)(2,1)S(1)} fusion(bf16[3200,768]{0,1:T(8,128)(2,1)} %bitcast.89, f32[3200]{0:T(1024)S(1)} %reduce, bf16[1024,3200]{1,0:T(8,128)(2,1)S(1)} %copy-done.2, f32[1024]{0:T(1024)S(1)} %add_sqrt_fusion), kind=kOutput, calls=%fused_computation.28 | convolution fusion | flops 5047058432 | bytes 13058560 | tf_op jit(solution)/shard_map/dot_general | solution.py:57
  208.0 2.0 copy-done.3
  210.8 123.1 %all-gather.7.cloned.1.call-done = bf16[1,1,1024,3200]{3,2,1,0:T(8,128)(2,1)} async-done(((bf16[1,1,128,3200]{3,2,1,0:T(8,128)(2,1)}), bf16[1,1,1024,3200]{3,2,1,0:T(8,128)(2,1)}) %all-gather.7.cloned.1.call-update) | async-done | bytes 6553616 | tf_op jit(solution)/shard_map/all_gather | solution.py:59
  333.9 5.0 fusion.15
  338.9 1.1 multiply_reduce_fusion.1
  340.1 1.3 multiply_convert_fusion.2
  342.6 1.0 fusion.28
  345.2 1.1 multiply_reduce_fusion.2
  346.3 1.3 multiply_convert_fusion.3
  348.1 0.8 fusion.24
  348.9 1.3 fusion.31
  351.2 5.9 convolution_convert_fusion
  357.1 2.8 multiply_reduce_fusion
  359.9 10.2 %divide_add_fusion = f32[1024,3200]{1,0:T(8,128)} fusion(bf16[1024,3200]{1,0:T(8,128)(2,1)S(1)} %convolution_convert_fusion, bf16[1024,3200]{1,0:T(8,128)(2,1)} %bitcast_dynamic-update-slice_fusion, f32[1024]{0:T(1024)S(1)} %broadcast_multiply_fusion, f32[1024]{0:T(1024)S(1)} %add_sqrt_fusion, f32[3200]{0:T(1024)S(1)} %reduce, bf16[1024,3200]{1,0:T(8,128)(2,1)S(1)} %bitcast.88), kind=kLoop, calls=%fused_computation.3 | loop fusion | flops 29491200 | bytes 32788992 | tf_op jit(solution)/shard_map/add | solution.py:18
  370.1 289.5 %all-reduce.3.cloned.1.call-done = f32[1024,3200]{1,0:T(8,128)} async-done(((f32[1024,3200]{1,0:T(8,128)}), f32[1024,3200]{1,0:T(8,128)}) %all-reduce.3.cloned.1.call-update) | async-done | bytes 13107216
  659.6 1.5 constant_dynamic-slice_fusion
  (41 shorter events, 6.9 us)
Async XLA Ops:
  6.5 327.4 %copy-start = (bf16[1,2,128,3200]{3,2,1,0:T(8,128)(2,1)S(1)}, bf16[1,2,128,3200]{3,2,1,0:T(8,128)(2,1)}, u32[]{:S(2)}) copy-start(bf16[1,2,128,3200]{3,2,1,0:T(8,128)(2,1)} %param.11) | copy-start | bytes 4915204
  6.5 188.0 %all-gather.5.cloned.1.call-start = ((), (), s32[]{:S(2)}) async-start(), calls=%async_computation | async-start | bytes 7372800 | tf_op jit(solution)/shard_map/all_gather | solution.py:54
  63.9 270.0 %all-gather.7.cloned.1.call-start = ((), (), s32[]{:S(2)}) async-start(), calls=%async_computation.1 | async-start | bytes 7372800 | tf_op jit(solution)/shard_map/all_gather | solution.py:59
  64.7 595.0 %all-reduce.3.cloned.1.call-start = ((), (), s32[]{:S(2)}) async-start(), calls=%async_computation.2 | async-start | bytes 26214400
  64.7 14.3 %copy-start.6 = (f32[1,3200]{1,0:T(1,128)S(1)}, f32[1,3200]{1,0:T(1,128)}, u32[]{:S(2)}) copy-start(f32[1,3200]{1,0:T(1,128)} %param.9) | copy-start | bytes 38404
  79.0 3.2 copy-start.5
  194.5 4.7 copy-start.2
  208.0 2.0 copy-start.3
  333.9 5.0 copy-start.4
  348.1 2.5 slice-start.2
  348.9 2.2 slice-start.3
  350.4 6.7 %slice-start = ((s8[6553600]{0:T(1024)(128)(4,1)}), s8[4194304]{0:T(1024)(128)(4,1)S(1)}, s32[]{:S(2)}) async-start(s8[6553600]{0:T(1024)(128)(4,1)} %bitcast.87), calls=%async_computation.3 | async-start | bytes 8388608
  351.2 6.0 slice-start.1
  370.1 291.1 %copy-start.1 = (bf16[1,2,128,3200]{3,2,1,0:T(8,128)(2,1)S(1)}, bf16[1,2,128,3200]{3,2,1,0:T(8,128)(2,1)}, u32[]{:S(2)}) copy-start(bf16[1,2,128,3200]{3,2,1,0:T(8,128)(2,1)} %param.11) | copy-start | bytes 4915204
Sparse Core Ops, SparseCore 0:
  64.0 130.4 all-gather.4
  196.3 137.5 all-gather.6
  370.2 289.3 all-reduce.2
where the time goes:
time: 668 us
  waiting for transfers between devices  525 us (79%)
  blocking collectives  53.6 us (8%)
  matrix products  27.6 us (4%)
  local copies, waits for them, and re-layouts  24.4 us (4%)
  other arithmetic  23.9 us (4%)
  between operations  13.4 us (2%)
    unnamed x4, waiting for transfers between devices  290 us
    all_gather x1, waiting for transfers between devices, on_device(): lax.all_gather(own_grad, 'tensor', axis=0, tiled=True)  123 us
    all_gather x1, waiting for transfers between devices, on_device(): all_inputs = lax.all_gather(inputs, 'tensor', axis=0, tiled=True)  111 us
    all_gather x1, blocking collectives, on_device(): shared = lax.all_gather(perturb, ('member', 'image'), axis=0, tiled=True)  53.6 us
    unnamed x24, local copies, waits for them, and re-layouts  18.8 us
  transfers between devices with their start and end apart: 3, of which 3 were waited for; matrix products, arithmetic and copies ran while one was open for 5% of the time, Pallas kernels for 0%

commit v1 on v0

--- a/solution.py
+++ b/solution.py
@@ -51,7 +51,9 @@
     score_scale = 1.0 / math.sqrt(head_size)
     shared = lax.all_gather(perturb, ("member", "image"), axis=0, tiled=True)
     inputs = (own_rows.astype(jnp.float32) + shared.astype(jnp.float32)).astype(jnp.bfloat16)
-    all_inputs = lax.all_gather(inputs, "tensor", axis=0, tiled=True)
+    all_inputs = jnp.concatenate(
+        lax.all_to_all(jnp.stack([inputs] * lax.axis_size("tensor")), "tensor", 0, 0), axis=0
+    )
     scaled_rows, spread = normalize(all_inputs)
     normed = (scaled_rows * gains).astype(jnp.bfloat16)
     packed = jnp.dot(normed, w_mat, preferred_element_type=jnp.float32).astype(jnp.bfloat16)

time: 668 us -> 601 us (0.90)
  waiting for transfers between devices: 525 us -> 442 us
  other arithmetic: 23.9 us -> 32.7 us
    all_to_all x0 -> x1, waiting for transfers between devices: none -> 117 us  [on_device(): lax.all_to_all(jnp.stack([inputs] * lax.axis_size('tensor')), 'tensor', 0...]
    all_gather x1 -> x0, waiting for transfers between devices: 111 us -> none  [on_device(): all_inputs = lax.all_gather(inputs, 'tensor', axis=0, tiled=True)]
    all_gather x1, waiting for transfers between devices: 123 us -> 41.7 us  [on_device(): lax.all_gather(own_grad, 'tensor', axis=0, tiled=True)]
    unnamed x4 -> x3, waiting for transfers between devices: 290 us -> 284 us
    unnamed x24 -> x22, local copies, waits for them, and re-layouts: 18.8 us -> 18.6 us
  transfers between devices with their start and end apart: 3 -> 3, of which waited for: 3 -> 3; matrix products, arithmetic and copies ran while one was open for 5% -> 6% of each run, Pallas kernels for 0% -> 0%
where the time goes in v1:
time: 601 us; the launch traced here: 600 us
  waiting for transfers between devices  442 us (74%)
  blocking collectives  53.6 us (9%)
  other arithmetic  32.7 us (5%)
  local copies, waits for them, and re-layouts  27.8 us (5%)
  matrix products  25 us (4%)
  between operations  13.7 us (2%)
    unnamed x3, waiting for transfers between devices  284 us
    all_to_all x1, waiting for transfers between devices, on_device(): lax.all_to_all(jnp.stack([inputs] * lax.axis_size('tensor')), 'tensor', 0...  117 us
    all_gather x1, blocking collectives, on_device(): shared = lax.all_gather(perturb, ('member', 'image'), axis=0, tiled=True)  53.6 us
    all_gather x1, waiting for transfers between devices, on_device(): lax.all_gather(own_grad, 'tensor', axis=0, tiled=True)  41.7 us
    unnamed x22, local copies, waits for them, and re-layouts  18.6 us
  transfers between devices with their start and end apart: 3, of which 3 were waited for; matrix products, arithmetic and copies ran while one was open for 6% of the time, Pallas kernels for 0%

profile of v1, /device:TPU:2, one launch (start us, length us, event | category | flops | bytes accessed | tf_op | source)
XLA Modules:
  0.0 600.1 jit_solution(12159936914293854829)
XLA Ops:
  6.5 53.6 %all-gather.1 = bf16[32,4,3200]{2,1,0:T(4,128)(2,1)} all-gather(bf16[1,4,3200]{2,1,0:T(4,128)(2,1)} %bitcast.113), channel_id=1, replica_groups=mesh['tensor'=8,'member'=4,'image'=8] {'member','image'}, dimensions={0}, use_global_device_ids=true | all-gather | bytes 844800 | tf_op jit(solution)/shard_map/all_gather | solution.py:52
  60.1 1.5 reshape.62
  61.7 1.3 fusion.10
  62.9 3.5 stack.44
  66.5 5.2 all-to-all-start
  72.5 14.2 %copy.8 = bf16[1,3200,2,3,128]{1,4,3,2,0:T(8,128)(2,1)} copy(bf16[1,3200,2,3,128]{4,2,3,1,0:T(2,128)(2,1)} %param.10) | data formatting | bytes 9830400 | tf_op args[4]
  86.7 3.2 broadcast_in_dim.2
  90.9 116.6 %all-to-all-done = bf16[8,128,3200]{2,1,0:T(8,128)(2,1)} async-done(((bf16[8,128,3200]{2,1,0:T(8,128)(2,1)}), bf16[8,128,3200]{2,1,0:T(8,128)(2,1)}, u32[]{:S(2)}, u32[]{:S(2)}) %all-to-all-start) | async-done | bytes 6553632 | tf_op jit(solution)/shard_map/all_to_all | solution.py:55
  207.5 4.4 multiply_reduce_fusion.1
  211.9 5.3 multiply_convert_fusion
  217.3 5.5 convolution_convert_fusion.1
  223.5 2.0 copy-done.2
  226.3 41.7 %all-gather.4.cloned.1.call-done = bf16[1,1,1024,3200]{3,2,1,0:T(8,128)(2,1)} async-done(((bf16[1,1,128,3200]{3,2,1,0:T(8,128)(2,1)}), bf16[1,1,1024,3200]{3,2,1,0:T(8,128)(2,1)}) %all-gather.4.cloned.1.call-update) | async-done | bytes 6553616 | tf_op jit(solution)/shard_map/all_gather | solution.py:61
  268.0 5.0 fusion.11
  273.0 1.1 multiply_reduce_fusion.2
  274.1 1.4 multiply_convert_fusion.1
  276.9 1.0 fusion.24
  279.4 1.1 multiply_reduce_fusion.3
  280.6 1.3 multiply_convert_fusion.2
  285.4 6.2 %convolution_convert_fusion = bf16[1024,3200]{1,0:T(8,128)(2,1)S(1)} fusion(bf16[1024,768]{0,1:T(8,128)(2,1)S(1)} %bitcast.112, bf16[3200,768]{0,1:T(8,128)(2,1)S(1)} %bitcast.103), kind=kOutput, calls=%fused_computation.6 | convolution fusion | flops 5036441600 | bytes 13041664 | tf_op jit(solution)/shard_map/dot_general | solution.py:88
  291.5 5.6 multiply_reduce_fusion
  297.2 11.5 %divide_add_fusion = f32[1024,3200]{1,0:T(8,128)} fusion(bf16[1024,3200]{1,0:T(8,128)(2,1)S(1)} %convolution_convert_fusion, bf16[1024,3200]{1,0:T(8,128)(2,1)} %bitcast_dynamic-update-slice_fusion, f32[1024]{0:T(1024)S(1)} %broadcast_multiply_fusion, f32[1024]{0:T(1024)S(1)} %get-tuple-element.5, f32[3200]{0:T(1024)S(1)} %reduce.1, ...), kind=kLoop, calls=%fused_computation.1 | loop fusion | flops 29491200 | bytes 32788992 | tf_op jit(solution)/shard_map/add | solution.py:18
  308.7 283.0 %all-reduce.3.cloned.1.call-done = f32[1024,3200]{1,0:T(8,128)} async-done(((f32[1024,3200]{1,0:T(8,128)}), f32[1024,3200]{1,0:T(8,128)}) %all-reduce.3.cloned.1.call-update) | async-done | bytes 13107216
  591.7 1.5 constant_dynamic-slice_fusion
  (40 shorter events, 9.6 us)
Async XLA Ops:
  6.5 261.4 %copy-start = (bf16[1,2,128,3200]{3,2,1,0:T(8,128)(2,1)S(1)}, bf16[1,2,128,3200]{3,2,1,0:T(8,128)(2,1)}, u32[]{:S(2)}) copy-start(bf16[1,2,128,3200]{3,2,1,0:T(8,128)(2,1)} %param.11) | copy-start | bytes 4915204
  66.5 141.0 %all-to-all-start = ((bf16[8,128,3200]{2,1,0:T(8,128)(2,1)}), bf16[8,128,3200]{2,1,0:T(8,128)(2,1)}, u32[]{:S(2)}, u32[]{:S(2)}) async-start(bf16[8,128,3200]{2,1,0:T(8,128)(2,1)} %stack.44), calls=%async_computation | async-start | bytes 13107200 | tf_op jit(solution)/shard_map/all_to_all | solution.py:55
  71.7 196.3 %all-gather.4.cloned.1.call-start = ((), (), s32[]{:S(2)}) async-start(), calls=%async_computation.1 | async-start | bytes 7372800 | tf_op jit(solution)/shard_map/all_gather | solution.py:61
  72.4 519.3 %all-reduce.3.cloned.1.call-start = ((), (), s32[]{:S(2)}) async-start(), calls=%async_computation.2 | async-start | bytes 26214400
  72.5 14.2 %copy-start.5 = (f32[1,3200]{1,0:T(1,128)S(1)}, f32[1,3200]{1,0:T(1,128)}, u32[]{:S(2)}) copy-start(f32[1,3200]{1,0:T(1,128)} %param.9) | copy-start | bytes 38404
  86.7 3.3 copy-start.4
  207.5 9.7 %slice-start = ((s8[4915200]{0:T(1024)(128)(4,1)}), s8[4194304]{0:T(1024)(128)(4,1)S(1)}, s32[]{:S(2)}) async-start(s8[4915200]{0:T(1024)(128)(4,1)} %bitcast.98), calls=%async_computation.3 | async-start | bytes 8388608
  211.9 5.4 slice-start.1
  223.5 2.0 copy-start.2
  268.0 5.0 copy-start.3
  282.3 2.2 slice-start.2
  283.1 2.2 slice-start.3
  308.7 284.6 %copy-start.1 = (bf16[1,2,128,3200]{3,2,1,0:T(8,128)(2,1)S(1)}, bf16[1,2,128,3200]{3,2,1,0:T(8,128)(2,1)}, u32[]{:S(2)}) copy-start(bf16[1,2,128,3200]{3,2,1,0:T(8,128)(2,1)} %param.11) | copy-start | bytes 4915204
Sparse Core Ops, SparseCore 0:
  74.3 193.6 all-gather.3
  308.8 282.8 all-reduce.2
